TPU v7x, 32 devices: a whole 2x2x4 slice. The times are simulated.
32 devices in a mesh: tok: 8 (over y, x, core), head: 4 (over z).
Axes of the slice: x: 2, y: 2, z: 4, core: 2. Of those that a mesh axis runs over, the one named last changes fastest.
Arguments:
- fast_query: bfloat16 [2, 1024, 2048], P(None, 'tok', 'head'), may hold values from -6 to 6
- fast_key: bfloat16 [2, 1024, 2048], P(None, 'tok', 'head'), may hold values from -6 to 6
- fast_value: bfloat16 [2, 1024, 2048], P(None, 'tok', 'head'), may hold values from -6 to 6
- fast_rate: float32 [2, 1024, 4], P(None, 'tok', 'head'), may hold values from 0.003125 to 0.03125
- fast_weights: bfloat16 [4, 512, 3, 512], P('head', 'tok'), may hold values from -0.25 to 0.25
- norm_gain: float32 [2048], P('head'), may hold values from 0.25 to 1.75
- key_value: bfloat16 [2, 1024, 512], P(None, 'tok', 'head'), may hold values from -450 to 450
Outputs:
- layer_output: bfloat16 [2, 1024, 2048], P(None, 'tok', 'head')
All inputs are finite; a program needn't handle non-finite values.
Results may differ from a plain program's by a relative error of at most 0.04.
The roundings to bfloat16 on the way count: a program that leaves them out, or rounds other values in their place, can miss the bound.
Values may be sent and summed in bfloat16 or wider, within the bound.
A program may use at most 64 MiB of HBM per device.

v0:
```python
import math

import jax
import jax.numpy as jnp
from jax import lax
from jax.sharding import PartitionSpec as P

WIN = 1024


EPSILON = 1e-06


def from_partner(block, axis, stride):
    count = lax.axis_size(axis)
    route = []
    for low in range(count):
        high = low | 1 << stride
        if high != low and high < count:
            route += [(low, high), (high, low)]
    return lax.ppermute(block, axis, route)


def passed_along(array, axis, by):
    length = lax.axis_size(axis)
    return lax.ppermute(array, axis, [(i, (i + by) % length) for i in range(length)])


def product(inputs, matrix):
    return jnp.dot(inputs, matrix, preferred_element_type=jnp.float32)


def fast_apply(inputs, weights):
    gate_value = product(inputs, weights[:, 0])
    up_value = product(inputs, weights[:, 1])
    hidden = (jax.nn.silu(gate_value) * up_value).astype(jnp.bfloat16)
    return product(hidden, weights[:, 2])


def backward_terms(key_in, value_in, rates, weights):
    gate_value = product(key_in, weights[:, 0])
    up_value = product(key_in, weights[:, 1])
    sigmoid_gate = jax.nn.sigmoid(gate_value)
    activated = gate_value * sigmoid_gate
    key_hidden = (activated * up_value).astype(jnp.bfloat16)
    scaled = (rates * value_in.astype(jnp.float32)).astype(jnp.bfloat16)
    backward = lax.dot_general(
        scaled, weights[:, 2], (((1,), (1,)), ((), ())), preferred_element_type=jnp.float32
    )
    gate_grad = (
        backward * up_value * sigmoid_gate * (1.0 + gate_value * (1.0 - sigmoid_gate))
    ).astype(jnp.bfloat16)
    up_grad = (backward * activated).astype(jnp.bfloat16)
    return (key_hidden, scaled, gate_grad, up_grad)


def gradient_rows(key_in, terms):
    key_hidden, scaled, gate_grad, up_grad = terms
    across = (((0,), (0,)), ((), ()))
    gate_rows = lax.dot_general(key_in, gate_grad, across, preferred_element_type=jnp.float32)
    up_rows = lax.dot_general(key_in, up_grad, across, preferred_element_type=jnp.float32)
    down_rows = lax.dot_general(key_hidden, scaled, across, preferred_element_type=jnp.float32)
    return jnp.stack([gate_rows, up_rows, down_rows], axis=1)


def renormed(previous, gradient):
    earlier = previous.astype(jnp.float32)
    updated = earlier + gradient
    factor = jnp.sqrt(jnp.mean(earlier * earlier, axis=-1, keepdims=True) + EPSILON) * lax.rsqrt(
        jnp.mean(updated * updated, axis=-1, keepdims=True) + EPSILON
    )
    return (updated * factor).astype(jnp.bfloat16)


def normalized(raw, gain_row):
    factor = lax.rsqrt(jnp.mean(raw * raw, axis=-1, keepdims=True) + EPSILON)
    return (raw * factor * gain_row).astype(jnp.bfloat16)


def attend(queries, key_block, value_block, allowed, head_size):
    tokens = queries.shape[0]
    per_head = queries.reshape(tokens, -1, head_size)
    scores = jnp.einsum(
        "qhd,kd->hqk", per_head, key_block, preferred_element_type=jnp.float32
    ) / math.sqrt(head_size)
    scores = jnp.where(allowed[None], scores, -1e30)
    row_max = jnp.max(scores, axis=-1, keepdims=True)
    lifted = jnp.exp(scores - row_max)
    weights = (lifted / jnp.sum(lifted, axis=-1, keepdims=True)).astype(jnp.bfloat16)
    mixed = jnp.einsum("hqk,kd->qhd", weights, value_block, preferred_element_type=jnp.float32)
    return mixed.reshape(tokens, -1)


def shards(fast_query, fast_key, fast_value, fast_rate, fast_weights, norm_gain, key_value):
    tokens = fast_query.shape[1]
    head_size = key_value.shape[2]
    place = lax.axis_index("tok")
    block_len = tokens * lax.axis_size("tok")
    own_rows = fast_weights[0]
    initial = lax.all_gather(own_rows, "tok", axis=0, tiled=True)
    terms = backward_terms(fast_key[0], fast_value[0], fast_rate[0], initial)
    gradient = lax.psum(gradient_rows(fast_key[0], terms), "tok")
    refreshed = renormed(initial, gradient)
    partner = from_partner(key_value, "head", 0)
    holds_key = lax.axis_index("head") % 2 == 0
    key_part = jnp.where(holds_key, key_value, partner)
    value_part = jnp.where(holds_key, partner, key_value)
    pair_stack = jnp.stack([key_part, value_part])
    reach = WIN // tokens
    arrived = []
    for distance in range(1, reach + 1):
        arrived.append(passed_along(pair_stack, "tok", distance))
    aligned = []
    for distance in range(reach, 0, -1):
        piece = arrived[distance - 1]
        aligned.append(jnp.where(place >= distance, piece, piece[:, 0:1]))
    aligned.append(pair_stack)
    window = jnp.concatenate(aligned, axis=2)
    span = window.shape[2]
    query_pos = lax.broadcasted_iota(jnp.int32, (tokens, span), 0)
    key_pos = lax.broadcasted_iota(jnp.int32, (tokens, span), 1) - reach * tokens
    offset = query_pos - key_pos
    inside = (offset >= 0) & (offset < WIN)

    def finish(block_index, matrices):
        fast_out = normalized(fast_apply(fast_query[block_index], matrices), norm_gain)
        allowed = inside & (block_index * block_len + place * tokens + key_pos >= 0)
        attended = attend(
            fast_out, window[0, block_index], window[1, block_index], allowed, head_size
        )
        return (fast_out.astype(jnp.float32) + attended).astype(jnp.bfloat16)

    first_final = finish(0, initial)
    second_final = finish(1, refreshed)
    return jnp.stack([first_final, second_final])


def solution(mesh):
    in_specs = (
        P(None, "tok", "head"),
        P(None, "tok", "head"),
        P(None, "tok", "head"),
        P(None, "tok", "head"),
        P("head", "tok", None, None),
        P("head"),
        P(None, "tok", "head"),
    )
    out_specs = P(None, "tok", "head")
    return jax.shard_map(shards, mesh=mesh, in_specs=in_specs, out_specs=out_specs, check_vma=False)
```

profile of v0, /device:TPU:0, one launch (start us, length us, event | category | flops | bytes accessed | tf_op | source)
XLA Modules:
  0.0 135.8 jit_solution(11874210293994285273)
XLA Ops:
  6.5 0.7 all-gather.3.cloned.1.call-update
  7.3 3.1 %collective-permute-start = (bf16[2,128,128]{2,1,0:T(8,128)(2,1)}, bf16[2,128,128]{2,1,0:T(8,128)(2,1)S(1)}, u32[]{:S(2)}, u32[]{:S(2)}) collective-permute-start(bf16[2,128,128]{2,1,0:T(8,128)(2,1)} %param.13), channel_id=1, source_target_pairs={{0,1},{1,0},{2,3},{3,2},{4,5},{5,4},{6,7},{7,6},{8,9},{9,8},{10,11... | collective-permute-start | bytes 196616 | tf_op jit(solution)/shard_map/ppermute | solution.py:21
  10.4 1.1 fusion.26
  11.5 1.3 collective-permute-done
  12.8 0.9 select_bitcast_fusion.1
  14.4 1.2 collective-permute-start.2
  15.6 1.7 %collective-permute-start.3 = (bf16[2,2,128,128]{3,2,1,0:T(8,128)(2,1)S(1)}, bf16[2,2,128,128]{3,2,1,0:T(8,128)(2,1)S(1)}, u32[]{:S(2)}, u32[]{:S(2)}) collective-permute-start(bf16[2,2,128,128]{3,2,1,0:T(8,128)(2,1)S(1)} %pad_maximum_fusion.2), channel_id=1, source_target_pairs={{0,24},{4,28},{8,0},{12,4},{16,8},{20,12},{24,16},{28,20},{1,25},{... | collective-permute-start | bytes 393224 | tf_op jit(solution)/shard_map/ppermute | solution.py:26
  17.6 1.5 %collective-permute-start.5 = (bf16[2,2,128,128]{3,2,1,0:T(8,128)(2,1)S(1)}, bf16[2,2,128,128]{3,2,1,0:T(8,128)(2,1)S(1)}, u32[]{:S(2)}, u32[]{:S(2)}) collective-permute-start(bf16[2,2,128,128]{3,2,1,0:T(8,128)(2,1)S(1)} %pad_maximum_fusion.2), channel_id=1, source_target_pairs={{0,16},{4,20},{8,24},{12,28},{16,0},{20,4},{24,8},{28,12},{1,17},{... | collective-permute-start | bytes 393224 | tf_op jit(solution)/shard_map/ppermute | solution.py:26
  19.3 1.5 %collective-permute-start.7 = (bf16[2,2,128,128]{3,2,1,0:T(8,128)(2,1)S(1)}, bf16[2,2,128,128]{3,2,1,0:T(8,128)(2,1)S(1)}, u32[]{:S(2)}, u32[]{:S(2)}) collective-permute-start(bf16[2,2,128,128]{3,2,1,0:T(8,128)(2,1)S(1)} %pad_maximum_fusion.2), channel_id=1, source_target_pairs={{0,8},{4,12},{8,16},{12,20},{16,24},{20,28},{24,0},{28,4},{1,9},{5... | collective-permute-start | bytes 393224 | tf_op jit(solution)/shard_map/ppermute | solution.py:26
  20.8 4.0 %collective-permute-done.3 = bf16[2,2,128,128]{3,2,1,0:T(8,128)(2,1)S(1)} collective-permute-done((bf16[2,2,128,128]{3,2,1,0:T(8,128)(2,1)S(1)}, bf16[2,2,128,128]{3,2,1,0:T(8,128)(2,1)S(1)}, u32[]{:S(2)}, u32[]{:S(2)}) %collective-permute-start.3) | collective-permute-done | bytes 131104 | tf_op jit(solution)/shard_map/ppermute | solution.py:26
  24.9 9.0 %collective-permute-done.5 = bf16[2,2,128,128]{3,2,1,0:T(8,128)(2,1)S(1)} collective-permute-done((bf16[2,2,128,128]{3,2,1,0:T(8,128)(2,1)S(1)}, bf16[2,2,128,128]{3,2,1,0:T(8,128)(2,1)S(1)}, u32[]{:S(2)}, u32[]{:S(2)}) %collective-permute-start.5) | collective-permute-done | bytes 131104 | tf_op jit(solution)/shard_map/ppermute | solution.py:26
  33.9 0.7 select_dynamic-update-slice_fusion.7
  34.6 0.7 select_dynamic-update-slice_fusion.6
  35.3 0.7 select_dynamic-update-slice_fusion.5
  36.0 0.7 select_dynamic-update-slice_fusion.4
  36.7 0.7 select_dynamic-update-slice_fusion.3
  37.4 0.7 select_dynamic-update-slice_fusion.2
  38.1 0.7 select_dynamic-update-slice_fusion.1
  38.9 3.4 %all-gather.3.cloned.1.call-done = bf16[1,512,3,512]{3,1,2,0:T(8,128)(2,1)} async-done(((bf16[1,64,3,512]{3,1,2,0:T(8,128)(2,1)}), bf16[1,512,3,512]{3,1,2,0:T(8,128)(2,1)}) %all-gather.3.cloned.1.call-update) | async-done | bytes 1572880 | tf_op jit(solution)/shard_map/all_gather | solution.py:100
  42.2 1.7 %copy.19 = bf16[1,512,3,512]{1,3,2,0:T(8,128)(2,1)S(1)} copy(bf16[1,512,3,512]{3,1,2,0:T(8,128)(2,1)} %all-gather.3.cloned.1.call-done) | data formatting | bytes 3145728 | tf_op jit(solution)/shard_map/all_gather | solution.py:100
  46.3 2.0 %pad_maximum_fusion = f32[512,3,512]{0,2,1:T(8,128)} fusion(f32[512,1,512]{0,2,1:T(8,128)S(1)} %convolution_bitcast_fusion, f32[512,1,512]{0,2,1:T(8,128)S(1)} %convolution_bitcast_fusion.1, f32[512,1,512]{0,2,1:T(8,128)S(1)} %convolution_bitcast_fusion.2), kind=kLoop, calls=%fused_computation.15 | loop fusion | flops 1572864 | bytes 6291456 | tf_op jit(solution)/shard_map/stack | solution.py:63
  48.4 0.7 select_dynamic-update-slice_fusion
  49.1 0.7 constant_dynamic-update-slice_fusion
  50.7 2.0 %fusion.124 = f32[4,128]{1,0:T(4,128)S(1)} fusion(pred[128,1152]{0,1:T(8,128)(4,1)S(1)} %get-tuple-element.9, bf16[2,2,1152,128]{3,2,1,0:T(8,128)(2,1)} %constant_dynamic-update-slice_fusion, f32[512]{0:T(512)S(1)} %copy-done.7, f32[128,512]{1,0:T(8,128)S(1)} %get-tuple-element.14, f32[128]{0:T(128)S(1)} %add_rsqrt_fusion.1), kind=kOutput, calls=%fused_computation.160 | convolution fusion | flops 153552000 | bytes 709120 | tf_op jit(solution)/shard_map/sub | solution.py:88
  52.7 2.4 %fusion.11 = f32[128,4,128]{2,0,1:T(8,128)S(1)} fusion(f32[4,128]{1,0:T(4,128)S(1)} %fusion.124, bf16[2,2,1152,128]{3,2,1,0:T(8,128)(2,1)} %constant_dynamic-update-slice_fusion, pred[128,1152]{0,1:T(8,128)(4,1)S(1)} %get-tuple-element.9, f32[512]{0:T(512)S(1)} %copy-done.7, f32[128,512]{1,0:T(8,128)S(1)} %get-tuple-element.14, f32[128]{0:T(128)S(1)} %add_rsqrt_fusion.1), kind=kOutput, calls=%fused_computation.23 | convolution fusion | flops 305137280 | bytes 1266176 | tf_op jit(solution)/shard_map/hqk,kd->qhd/dot_general | solution.py:90
  55.3 62.6 %all-reduce.2.cloned.1.call-done = f32[512,3,512]{0,2,1:T(8,128)} async-done(((f32[512,3,512]{0,2,1:T(8,128)}), f32[512,3,512]{0,2,1:T(8,128)}) %all-reduce.2.cloned.1.call-update) | async-done | bytes 3145744 | tf_op jit(solution)/shard_map/psum | solution.py:102
  117.9 2.7 %fusion.10 = (f32[512,3]{0,1:T(4,128)S(1)}, f32[512,3]{0,1:T(4,128)S(1)}) fusion(bf16[1,512,3,512]{1,3,2,0:T(8,128)(2,1)S(1)} %copy.19, f32[512,3,512]{0,2,1:T(8,128)} %all-reduce.2.cloned.1.call-done), kind=kLoop, calls=%fused_computation.14 | loop fusion | flops 4715520 | bytes 4730880 | tf_op jit(solution)/shard_map/reduce_sum | solution.py:69
  120.8 0.7 multiply_convert_fusion
  122.1 1.5 %multiply_reduce_fusion.1 = (f32[128]{0:T(128)S(1)}, f32[128,512]{1,0:T(8,128)S(1)}) fusion(bf16[512,3,512]{0,2,1:T(8,128)(2,1)S(1)} %multiply_convert_fusion, f32[128,512]{1,0:T(8,128)S(1)} %convolution_bitcast_fusion.4, bf16[2,128,512]{2,1,0:T(8,128)(2,1)} %param.7), kind=kOutput, calls=%fused_computation.61 | convolution fusion | flops 134741888 | bytes 1704448 | tf_op jit(solution)/shard_map/dot_general | solution.py:30
  123.8 1.9 %fusion.129 = f32[4,128]{1,0:T(4,128)S(1)} fusion(pred[128,1152]{0,1:T(8,128)(4,1)S(1)} %get-tuple-element.10, bf16[2,2,1152,128]{3,2,1,0:T(8,128)(2,1)} %constant_dynamic-update-slice_fusion, bf16[16,4,8,128]{3,2,1,0:T(8,128)(2,1)S(1)} %get-tuple-element.12), kind=kOutput, calls=%fused_computation.161 | convolution fusion | flops 153355392 | bytes 575488 | tf_op jit(solution)/shard_map/sub | solution.py:88
  125.6 2.3 %fusion.12 = f32[128,4,128]{2,0,1:T(8,128)S(1)} fusion(f32[4,128]{1,0:T(4,128)S(1)} %fusion.129, bf16[2,2,1152,128]{3,2,1,0:T(8,128)(2,1)} %constant_dynamic-update-slice_fusion, pred[128,1152]{0,1:T(8,128)(4,1)S(1)} %get-tuple-element.10, bf16[16,4,8,128]{3,2,1,0:T(8,128)(2,1)S(1)} %get-tuple-element.12), kind=kOutput, calls=%fused_computation.24 | convolution fusion | flops 304940672 | bytes 1132544 | tf_op jit(solution)/shard_map/hqk,kd->qhd/dot_general | solution.py:90
  128.2 0.7 pad_maximum_fusion.1
  (63 shorter events, 5.8 us)
Async XLA Ops:
  6.5 35.7 %all-gather.3.cloned.1.call-start = ((), (), s32[]{:S(2)}) async-start(), calls=%async_computation.1 | async-start | bytes 1769472 | tf_op jit(solution)/shard_map/all_gather | solution.py:100
  7.3 110.7 %all-reduce.2.cloned.1.call-start = ((), (), s32[]{:S(2)}) async-start(), calls=%async_computation | async-start | bytes 6291456 | tf_op jit(solution)/shard_map/psum | solution.py:102
  7.3 5.5 %collective-permute-start = (bf16[2,128,128]{2,1,0:T(8,128)(2,1)}, bf16[2,128,128]{2,1,0:T(8,128)(2,1)S(1)}, u32[]{:S(2)}, u32[]{:S(2)}) collective-permute-start(bf16[2,128,128]{2,1,0:T(8,128)(2,1)} %param.13), channel_id=1, source_target_pairs={{0,1},{1,0},{2,3},{3,2},{4,5},{5,4},{6,7},{7,6},{8,9},{9,8},{10,11... | collective-permute-start | bytes 196616 | tf_op jit(solution)/shard_map/ppermute | solution.py:21
  13.7 5.4 %collective-permute-start.1 = (bf16[2,2,128,128]{3,2,1,0:T(8,128)(2,1)S(1)}, bf16[2,2,128,128]{3,2,1,0:T(8,128)(2,1)S(1)}, u32[]{:S(2)}, u32[]{:S(2)}) collective-permute-start(bf16[2,2,128,128]{3,2,1,0:T(8,128)(2,1)S(1)} %pad_maximum_fusion.2), channel_id=1, source_target_pairs={{0,0},{4,4},{8,8},{12,12},{16,16},{20,20},{24,24},{28,28},{1,1},{5... | collective-permute-start | bytes 393224 | tf_op jit(solution)/shard_map/ppermute | solution.py:26
  14.4 4.9 %collective-permute-start.2 = (bf16[2,2,128,128]{3,2,1,0:T(8,128)(2,1)S(1)}, bf16[2,2,128,128]{3,2,1,0:T(8,128)(2,1)S(1)}, u32[]{:S(2)}, u32[]{:S(2)}) collective-permute-start(bf16[2,2,128,128]{3,2,1,0:T(8,128)(2,1)S(1)} %pad_maximum_fusion.2), channel_id=1, source_target_pairs={{0,28},{4,0},{8,4},{12,8},{16,12},{20,16},{24,20},{28,24},{1,29},{... | collective-permute-start | bytes 393224 | tf_op jit(solution)/shard_map/ppermute | solution.py:26
  15.6 9.2 %collective-permute-start.3 = (bf16[2,2,128,128]{3,2,1,0:T(8,128)(2,1)S(1)}, bf16[2,2,128,128]{3,2,1,0:T(8,128)(2,1)S(1)}, u32[]{:S(2)}, u32[]{:S(2)}) collective-permute-start(bf16[2,2,128,128]{3,2,1,0:T(8,128)(2,1)S(1)} %pad_maximum_fusion.2), channel_id=1, source_target_pairs={{0,24},{4,28},{8,0},{12,4},{16,8},{20,12},{24,16},{28,20},{1,25},{... | collective-permute-start | bytes 393224 | tf_op jit(solution)/shard_map/ppermute | solution.py:26
  17.3 7.5 %collective-permute-start.4 = (bf16[2,2,128,128]{3,2,1,0:T(8,128)(2,1)S(1)}, bf16[2,2,128,128]{3,2,1,0:T(8,128)(2,1)S(1)}, u32[]{:S(2)}, u32[]{:S(2)}) collective-permute-start(bf16[2,2,128,128]{3,2,1,0:T(8,128)(2,1)S(1)} %pad_maximum_fusion.2), channel_id=1, source_target_pairs={{0,20},{4,24},{8,28},{12,0},{16,4},{20,8},{24,12},{28,16},{1,21},{... | collective-permute-start | bytes 393224 | tf_op jit(solution)/shard_map/ppermute | solution.py:26
  17.6 16.2 %collective-permute-start.5 = (bf16[2,2,128,128]{3,2,1,0:T(8,128)(2,1)S(1)}, bf16[2,2,128,128]{3,2,1,0:T(8,128)(2,1)S(1)}, u32[]{:S(2)}, u32[]{:S(2)}) collective-permute-start(bf16[2,2,128,128]{3,2,1,0:T(8,128)(2,1)S(1)} %pad_maximum_fusion.2), channel_id=1, source_target_pairs={{0,16},{4,20},{8,24},{12,28},{16,0},{20,4},{24,8},{28,12},{1,17},{... | collective-permute-start | bytes 393224 | tf_op jit(solution)/shard_map/ppermute | solution.py:26
  19.2 14.7 %collective-permute-start.6 = (bf16[2,2,128,128]{3,2,1,0:T(8,128)(2,1)S(1)}, bf16[2,2,128,128]{3,2,1,0:T(8,128)(2,1)S(1)}, u32[]{:S(2)}, u32[]{:S(2)}) collective-permute-start(bf16[2,2,128,128]{3,2,1,0:T(8,128)(2,1)S(1)} %pad_maximum_fusion.2), channel_id=1, source_target_pairs={{0,12},{4,16},{8,20},{12,24},{16,28},{20,0},{24,4},{28,8},{1,13},{... | collective-permute-start | bytes 393224 | tf_op jit(solution)/shard_map/ppermute | solution.py:26
  19.3 14.6 %collective-permute-start.7 = (bf16[2,2,128,128]{3,2,1,0:T(8,128)(2,1)S(1)}, bf16[2,2,128,128]{3,2,1,0:T(8,128)(2,1)S(1)}, u32[]{:S(2)}, u32[]{:S(2)}) collective-permute-start(bf16[2,2,128,128]{3,2,1,0:T(8,128)(2,1)S(1)} %pad_maximum_fusion.2), channel_id=1, source_target_pairs={{0,8},{4,12},{8,16},{12,20},{16,24},{20,28},{24,0},{28,4},{1,9},{5... | collective-permute-start | bytes 393224 | tf_op jit(solution)/shard_map/ppermute | solution.py:26
  24.8 23.5 %collective-permute-start.8 = (bf16[2,2,128,128]{3,2,1,0:T(8,128)(2,1)S(1)}, bf16[2,2,128,128]{3,2,1,0:T(8,128)(2,1)S(1)}, u32[]{:S(2)}, u32[]{:S(2)}) collective-permute-start(bf16[2,2,128,128]{3,2,1,0:T(8,128)(2,1)S(1)} %pad_maximum_fusion.2), channel_id=1, source_target_pairs={{0,4},{4,8},{8,12},{12,16},{16,20},{20,24},{24,28},{28,0},{1,5},{5... | collective-permute-start | bytes 393224 | tf_op jit(solution)/shard_map/ppermute | solution.py:26
  38.9 5.1 %copy-start.1 = (bf16[2,128,512]{2,1,0:T(8,128)(2,1)S(1)}, bf16[2,128,512]{2,1,0:T(8,128)(2,1)}, u32[]{:S(2)}) copy-start(bf16[2,128,512]{2,1,0:T(8,128)(2,1)} %param.8) | copy-start | bytes 786436
  43.9 1.0 copy-start.2
  48.3 1.4 %copy-start.5 = (bf16[2,128,512]{2,1,0:T(8,128)(2,1)S(1)}, bf16[2,128,512]{2,1,0:T(8,128)(2,1)}, u32[]{:S(2)}) copy-start(bf16[2,128,512]{2,1,0:T(8,128)(2,1)} %param.7) | copy-start | bytes 786436
  50.1 0.7 copy-start.7
  50.7 2.1 %copy-start.3 = (f32[128,512]{1,0:T(8,128)}, f32[128,512]{1,0:T(8,128)S(1)}, u32[]{:S(2)}) copy-start(f32[128,512]{1,0:T(8,128)S(1)} %get-tuple-element.14) | copy-start | bytes 786436
  50.7 2.0 %copy-start.9 = (f32[128]{0:T(128)}, f32[128]{0:T(128)S(1)}, u32[]{:S(2)}) copy-start(f32[128]{0:T(128)S(1)} %add_rsqrt_fusion.1) | copy-start | bytes 1540
  117.9 2.8 %copy-start = (f32[512,3,512]{0,2,1:T(8,128)S(1)}, f32[512,3,512]{0,2,1:T(8,128)}, u32[]{:S(2)}) copy-start(f32[512,3,512]{0,2,1:T(8,128)} %all-reduce.2.cloned.1.call-done) | copy-start | bytes 9437188
  120.8 0.9 copy-start.6
  122.0 1.6 %copy-start.4 = (f32[128,512]{1,0:T(8,128)S(1)}, f32[128,512]{1,0:T(8,128)}, u32[]{:S(2)}) copy-start(f32[128,512]{1,0:T(8,128)} %copy-done.3) | copy-start | bytes 786436
  122.0 1.6 %copy-start.8 = (f32[512]{0:T(512)S(1)}, f32[512]{0:T(512)}, u32[]{:S(2)}) copy-start(f32[512]{0:T(512)} %param.12) | copy-start | bytes 6148
  122.0 1.6 %copy-start.10 = (f32[128]{0:T(128)S(1)}, f32[128]{0:T(128)}, u32[]{:S(2)}) copy-start(f32[128]{0:T(128)} %copy-done.9) | copy-start | bytes 1540
Sparse Core Ops, SparseCore 0:
  9.3 32.9 all-gather.2
  48.4 69.4 all-reduce.1
where the time goes:
time: 136 us
  waiting for transfers between devices  81 us (60%)
  other arithmetic  14.6 us (11%)
  between operations  13.8 us (10%)
  matrix products  13.4 us (10%)
  starting transfers between devices  9.55 us (7%)
  local copies, waits for them, and re-layouts  3.48 us (3%)
    psum x1, waiting for transfers between devices, shards(): gradient = lax.psum(gradient_rows(fast_key[0], terms), 'tok')  62.6 us
    ppermute x8, waiting for transfers between devices, passed_along(): lax.ppermute(array, axis, [(i, (i + by) % length) for i in range(length)])  13 us
    ppermute x8, starting transfers between devices, passed_along(): lax.ppermute(array, axis, [(i, (i + by) % length) for i in range(length)])  6.42 us
    unnamed x8, other arithmetic  5.63 us
    dot_general x2, matrix products, attend(): jnp.einsum('hqk,kd->qhd', weights, value_block, preferred_element_type=jn...  4.77 us
    sub x2, matrix products, attend(): lifted = jnp.exp(scores - row_max)  3.86 us
    all_gather x1, waiting for transfers between devices, shards(): initial = lax.all_gather(own_rows, 'tok', axis=0, tiled=True)  3.35 us
    dot_general x6, matrix products, product(): return jnp.dot(inputs, matrix, preferred_element_type=jnp.float32)  3.34 us
  transfers between devices with their start and end apart: 11, of which 5 were waited for; matrix products, arithmetic and copies ran while one was open for 15% of the time, Pallas kernels for 0%

commit v1 on v0

--- a/solution.py
+++ b/solution.py
@@ -3,6 +3,8 @@
 import jax
 import jax.numpy as jnp
 from jax import lax
+from jax.experimental import pallas as pl
+from jax.experimental.pallas import tpu as pltpu
 from jax.sharding import PartitionSpec as P
 
 WIN = 1024
@@ -134,6 +136,286 @@
     second_final = finish(1, refreshed)
     return jnp.stack([first_final, second_final])
 
+MESH = pl.DeviceIdType.MESH
+ALONG_ROWS = (((0,), (0,)), ((), ()))
+ALONG_COLUMNS = (((1,), (1,)), ((), ()))
+
+
+def dot_along(left, right, dims):
+    return lax.dot_general(left, right, dims, preferred_element_type=jnp.float32)
+
+
+def mixed_heads(fast_out, keys, values, valid):
+    tokens = fast_out.shape[0]
+    size = keys[0].shape[1]
+    heads = fast_out.shape[1] // size
+    stacked = jnp.concatenate([fast_out[:, h * size : (h + 1) * size] for h in range(heads)], axis=0)
+    scale = math.log2(math.e) / math.sqrt(size)
+    scores = [dot_along(stacked, part, ALONG_COLUMNS) for part in keys]
+    pieces = []
+    for h in range(heads):
+        masked = [
+            jnp.where(ok, s[h * tokens : (h + 1) * tokens], -1e30) for s, ok in zip(scores, valid)
+        ]
+        top = jnp.max(masked[0], axis=-1, keepdims=True)
+        for more in masked[1:]:
+            top = jnp.maximum(top, jnp.max(more, axis=-1, keepdims=True))
+        lifted = [jnp.exp2((part - top) * scale) for part in masked]
+        total = jnp.sum(lifted[0], axis=-1, keepdims=True)
+        for more in lifted[1:]:
+            total = total + jnp.sum(more, axis=-1, keepdims=True)
+        inverse = 1.0 / total
+        pieces.append([(part * inverse).astype(jnp.bfloat16) for part in lifted])
+    mixed = None
+    for i, part in enumerate(values):
+        weights = jnp.concatenate([piece[i] for piece in pieces], axis=0)
+        term = product(weights, part)
+        mixed = term if mixed is None else mixed + term
+    return jnp.concatenate([mixed[h * tokens : (h + 1) * tokens] for h in range(heads)], axis=1)
+
+
+def whole_kernel(
+    query_ref, key_ref, value_ref, rate_ref, weight_ref, gain_ref, kv_ref, out_ref,
+    w_buf, k_buf, s_buf, kv_buf, hidden_buf, gates_buf, new_buf, merged,
+    send_sem, recv_sem, z_send, z_recv,
+):
+    me = lax.axis_index("tok")
+    head = lax.axis_index("head")
+    kind = lax.rem(head, 2)
+    core = lax.rem(me, 2)
+    first_hop = jnp.where(core == 0, 2, 4)
+    second_hop = 6 - first_hop
+    sibling = me ^ 1
+    near, far = me ^ first_hop, me ^ second_hop
+    opposite = me ^ 6
+    opposite_head = head ^ 1
+    barrier = pltpu.get_barrier_semaphore()
+    for there in (sibling, near, far):
+        pl.semaphore_signal(barrier, inc=1, device_id=(there, head), device_id_type=MESH)
+    pl.semaphore_signal(barrier, inc=1, device_id=(me, opposite_head), device_id_type=MESH)
+
+    tokens = key_ref.shape[1]
+    depth = weight_ref.shape[0]
+    hd = key_ref.shape[2]
+    size = kv_ref.shape[2]
+
+    def rows(owner, count):
+        return pl.ds(pl.multiple_of(owner * count, count), count)
+
+    own = rows(me, tokens)
+    w_buf[rows(me, depth)] = weight_ref[...]
+    k_buf[own] = key_ref[0]
+    s_buf[own] = (rate_ref[0] * value_ref[0].astype(jnp.float32)).astype(jnp.bfloat16)
+    kv_buf[kind, :, own] = kv_ref[...]
+
+    def part_of(item, owner):
+        if item == 0:
+            return w_buf.at[rows(owner, depth)]
+        if item == 1:
+            return kv_buf.at[kind, :, rows(owner, tokens)]
+        if item == 2:
+            return k_buf.at[rows(owner, tokens)]
+        if item == 3:
+            return s_buf.at[rows(owner, tokens)]
+        return kv_buf.at[1 - kind, :, rows(owner, tokens)]
+
+    owners = [
+        me, near, far, opposite,
+        sibling, sibling ^ 2, sibling ^ 4, sibling ^ 6,
+    ]
+    started = []
+
+    def send(item, source, target, slot):
+        number = len(started)
+        copy = pltpu.make_async_remote_copy(
+            src_ref=part_of(item, owners[source]),
+            dst_ref=part_of(item, owners[source]),
+            send_sem=send_sem.at[number],
+            recv_sem=recv_sem.at[item, slot],
+            device_id=(target, head),
+            device_id_type=MESH,
+        )
+        copy.start()
+        started.append(copy)
+
+    across = []
+
+    def send_across(source):
+        ref = part_of(1, owners[source])
+        copy = pltpu.make_async_remote_copy(
+            src_ref=ref, dst_ref=ref, send_sem=z_send.at[source], recv_sem=z_recv.at[source],
+            device_id=(me, opposite_head), device_id_type=MESH,
+        )
+        copy.start()
+        across.append(copy)
+
+    def arrived(item, slot):
+        ref = part_of(item, owners[slot])
+        pltpu.make_async_remote_copy(
+            src_ref=ref, dst_ref=ref, send_sem=send_sem.at[0], recv_sem=recv_sem.at[item, slot],
+            device_id=(sibling, head), device_id_type=MESH,
+        ).wait_recv()
+
+    def arrived_across(source):
+        ref = part_of(4, owners[source])
+        pltpu.make_async_remote_copy(
+            src_ref=ref, dst_ref=ref, send_sem=z_send.at[0], recv_sem=z_recv.at[source],
+            device_id=(me, opposite_head), device_id_type=MESH,
+        ).wait_recv()
+
+    side = {0: 4, 1: jnp.where(core == 0, 5, 6), 2: jnp.where(core == 0, 6, 5), 3: 7}
+
+    def to_sibling(item, source):
+        send(item, source, sibling, side[source])
+
+    def pass_on(item, source):
+        arrived(item, source)
+        if source == 1:
+            send(item, 1, far, 3)
+        to_sibling(item, source)
+
+    pl.semaphore_wait(barrier, 4)
+    for item in (0, 1, 2, 3):
+        send(item, 0, near, 1)
+        send(item, 0, far, 2)
+        to_sibling(item, 0)
+        if item == 1:
+            send_across(0)
+
+    pass_on(0, 1)
+    pass_on(0, 2)
+    pass_on(1, 1)
+    send_across(1)
+    pass_on(1, 2)
+    send_across(2)
+    pass_on(0, 3)
+    for slot in range(4, 8):
+        arrived(0, slot)
+
+    gain = gain_ref[...]
+
+    def rms(total):
+        return lax.rsqrt(jnp.mean(total * total, axis=-1, keepdims=True) + EPSILON)
+
+    def applied(block, buf):
+        both = product(query_ref[block], buf[:, : 2 * hd])
+        gate_value, up_value = both[:, :hd], both[:, hd:]
+        hidden = (jax.nn.silu(gate_value) * up_value).astype(jnp.bfloat16)
+        raw = product(hidden, buf[:, 2 * hd :])
+        return (raw * rms(raw) * gain).astype(jnp.bfloat16)
+
+    fast_first = applied(0, w_buf)
+
+    def terms(chip):
+        span = rows(chip, 2 * tokens)
+        both = product(k_buf[span], w_buf[:, : 2 * hd])
+        gate_value, up_value = both[:, :hd], both[:, hd:]
+        sig = jax.nn.sigmoid(gate_value)
+        act = gate_value * sig
+        hidden_buf[span] = (act * up_value).astype(jnp.bfloat16)
+        backward = dot_along(s_buf[span], w_buf[:, 2 * hd :], ALONG_COLUMNS)
+        gates_buf[span, :hd] = (
+            backward * up_value * sig * (1.0 + gate_value * (1.0 - sig))
+        ).astype(jnp.bfloat16)
+        gates_buf[span, hd:] = (backward * act).astype(jnp.bfloat16)
+
+    chip = me // 2
+    arrived(2, 4)
+    arrived(3, 4)
+    pass_on(2, 1)
+    pass_on(3, 1)
+    terms(chip)
+    pass_on(2, 2)
+    pass_on(3, 2)
+    pass_on(1, 3)
+    send_across(3)
+    for source in range(4):
+        arrived_across(source)
+        to_sibling(4, source)
+    for slot in (5, 6):
+        arrived(2, slot)
+        arrived(3, slot)
+    terms(chip ^ 1)
+    terms(chip ^ 2)
+    for slot in range(4, 8):
+        arrived(1, slot)
+        arrived(4, slot)
+    pass_on(2, 3)
+    pass_on(3, 3)
+
+    length = k_buf.shape[0]
+    query_pos = me * tokens + lax.broadcasted_iota(jnp.int32, (tokens, length), 0)
+    key_pos = lax.broadcasted_iota(jnp.int32, (tokens, length), 1)
+    mixed = mixed_heads(fast_first, [kv_buf[0, 0]], [kv_buf[1, 0]], [key_pos <= query_pos])
+    out_ref[0] = (fast_first.astype(jnp.float32) + mixed).astype(jnp.bfloat16)
+
+    arrived(2, 7)
+    arrived(3, 7)
+    terms(chip ^ 3)
+
+    def renewed(part, gradient):
+        columns = slice(part * hd, (part + 1) * hd)
+        earlier = w_buf[:, columns].astype(jnp.float32)
+        updated = earlier + gradient
+        factor = jnp.sqrt(jnp.mean(earlier * earlier, axis=-1, keepdims=True) + EPSILON) * rms(updated)
+        new_buf[:, columns] = (updated * factor).astype(jnp.bfloat16)
+
+    both = dot_along(k_buf[...], gates_buf[...], ALONG_ROWS)
+    renewed(0, both[:, :hd])
+    renewed(1, both[:, hd:])
+    renewed(2, dot_along(hidden_buf[...], s_buf[...], ALONG_ROWS))
+
+    fast_second = applied(1, new_buf)
+    for shard in range(length // tokens):
+        place = slice(shard * tokens, (shard + 1) * tokens)
+        block = jnp.where(shard < me, 1, 0)
+        merged[0, place] = kv_buf[0, block, place]
+        merged[1, place] = kv_buf[1, block, place]
+    near_query = lax.broadcasted_iota(jnp.int32, (tokens, tokens), 0)
+    near_key = lax.broadcasted_iota(jnp.int32, (tokens, tokens), 1)
+    mixed = mixed_heads(
+        fast_second,
+        [merged[0], kv_buf[0, 1, own]],
+        [merged[1], kv_buf[1, 1, own]],
+        [(key_pos < me * tokens) | (key_pos > query_pos), near_key <= near_query],
+    )
+    out_ref[1] = (fast_second.astype(jnp.float32) + mixed).astype(jnp.bfloat16)
+    for copy in started + across:
+        copy.wait_send()
+
+
+def gathered_shards(fast_query, fast_key, fast_value, fast_rate, fast_weights, norm_gain, key_value):
+    members = lax.axis_size("tok")
+    _, depth, parts, hd = fast_weights.shape
+    _, tokens, size = key_value.shape
+    length = members * tokens
+    weights = fast_weights[0].reshape(depth, parts * hd)
+    sends = 4 * (members - 1) + members // 2
+    bf16 = jnp.bfloat16
+    return pl.pallas_call(
+        whole_kernel,
+        out_shape=jax.ShapeDtypeStruct(fast_query.shape, bf16),
+        in_specs=[pl.BlockSpec(memory_space=pltpu.VMEM)] * 7,
+        out_specs=pl.BlockSpec(memory_space=pltpu.VMEM),
+        scratch_shapes=[
+            pltpu.VMEM((members * depth, parts * hd), bf16),
+            pltpu.VMEM((length, hd), bf16),
+            pltpu.VMEM((length, hd), bf16),
+            pltpu.VMEM((2, 2, length, size), bf16),
+            pltpu.VMEM((length, hd), bf16),
+            pltpu.VMEM((length, 2 * hd), bf16),
+            pltpu.VMEM((members * depth, parts * hd), bf16),
+            pltpu.VMEM((2, length, size), bf16),
+            pltpu.SemaphoreType.DMA((sends,)),
+            pltpu.SemaphoreType.DMA((5, members)),
+            pltpu.SemaphoreType.DMA((members // 2,)),
+            pltpu.SemaphoreType.DMA((members // 2,)),
+        ],
+        compiler_params=pltpu.CompilerParams(
+            collective_id=0, has_side_effects=True, vmem_limit_bytes=56 * 1024 * 1024
+        ),
+    )(fast_query, fast_key, fast_value, fast_rate, weights, norm_gain[None], key_value)
+
 
 def solution(mesh):
     in_specs = (
@@ -146,4 +428,5 @@
         P(None, "tok", "head"),
     )
     out_specs = P(None, "tok", "head")
-    return jax.shard_map(shards, mesh=mesh, in_specs=in_specs, out_specs=out_specs, check_vma=False)
+    plan = gathered_shards if mesh.shape["tok"] == 8 else shards
+    return jax.shard_map(plan, mesh=mesh, in_specs=in_specs, out_specs=out_specs, check_vma=False)

time: 136 us -> 39.7 us (0.29)
  waiting for transfers between devices: 81 us -> 0 us
  Pallas kernels: 0 us -> 34.5 us
  other arithmetic: 14.6 us -> 0 us
  between operations: 13.8 us -> 0.01 us
  matrix products: 13.4 us -> 0 us
  starting transfers between devices: 9.55 us -> 0 us
  local copies, waits for them, and re-layouts: 3.48 us -> 4.97 us
    psum x1 -> x0, waiting for transfers between devices: 62.6 us -> none  [shards(): gradient = lax.psum(gradient_rows(fast_key[0], terms), 'tok')]
    pallas_call x0 -> x1, Pallas kernels: none -> 34.5 us  [gathered_shards(): pl.pallas_call(whole_kernel, out_shape=jax.ShapeDtypeStruct(fast_query.sh...]
    ppermute x9 -> x0, waiting for transfers between devices: 14.4 us -> none  [the longest x8 13 us: passed_along(): lax.ppermute(array, axis, [(i, (i + by) % length) for i in range(length)])]
    ppermute x9 -> x0, starting transfers between devices: 9.51 us -> none  [the longest x8 6.42 us: passed_along(): lax.ppermute(array, axis, [(i, (i + by) % length) for i in range(length)])]
    dot_general x12 -> x0, matrix products: 9.5 us -> none  [the longest x2 4.77 us: attend(): jnp.einsum('hqk,kd->qhd', weights, value_block, preferred_element_type=jn...]
    unnamed x8 -> x0, other arithmetic: 5.63 us -> none
    unnamed x22 -> x6, local copies, waits for them, and re-layouts: 0.79 us -> 4.97 us
    sub x2 -> x0, matrix products: 3.86 us -> none  [attend(): lifted = jnp.exp(scores - row_max)]
  transfers between devices with their start and end apart: 11 -> 0, of which waited for: 5 -> 0; matrix products, arithmetic and copies ran while one was open for 15% -> 0% of each run, Pallas kernels for 0% -> 0%
where the time goes in v1:
time: 39.7 us; the launch traced here: 39.5 us
  Pallas kernels  34.5 us (87%)
  local copies, waits for them, and re-layouts  4.97 us (13%)
    pallas_call x1, Pallas kernels, gathered_shards(): pl.pallas_call(whole_kernel, out_shape=jax.ShapeDtypeStruct(fast_query.sh...  34.5 us
    unnamed x6, local copies, waits for them, and re-layouts  4.97 us

profile of v1, /device:TPU:0, one launch (start us, length us, event | category | flops | bytes accessed | tf_op | source)
XLA Modules:
  0.0 39.5 jit_solution(9686641246010554172)
XLA Ops:
  0.0 0.0 copy-start
  0.0 0.7 %copy-done = f32[2,128,1]{1,2,0:T(1,128)S(1)} copy-done((f32[2,128,1]{1,2,0:T(1,128)S(1)}, f32[2,128,1]{1,2,0:T(1,128)}, u32[]{:S(2)}) %copy-start) | copy-done | bytes 1048
  0.7 0.8 %copy.11.rate_ref = f32[2,128,1]{2,1,0:T(8,128)} copy(f32[2,128,1]{1,2,0:T(1,128)S(1)} %copy-done) | data formatting | bytes 2048 | tf_op args[3]
  1.5 1.1 %copy.10 = bf16[1,64,3,512]{3,2,1,0:T(4,128)(2,1)S(1)} copy(bf16[1,64,3,512]{3,1,2,0:T(8,128)(2,1)} %param.11) | data formatting | bytes 393216 | tf_op args[4]
  2.6 0.7 %copy.12 = bf16[8,8,3,512]{3,1,2,0:T(8,128)(2,1)} copy(bf16[8,8,3,512]{3,2,1,0:T(4,128)(2,1)S(1)} %bitcast.4) | data formatting | bytes 393216
  3.3 34.5 %shard_map.73 = bf16[2,128,512]{2,1,0:T(8,128)(2,1)} custom-call(bf16[2,128,512]{2,1,0:T(8,128)(2,1)} %query_ref.1, bf16[2,128,512]{2,1,0:T(8,128)(2,1)} %key_ref.1, bf16[2,128,512]{2,1,0:T(8,128)(2,1)} %value_ref.1, f32[2,128,1]{2,1,0:T(8,128)} %copy.11.rate_ref, bf16[64,1536]{1,0:T(8,128)(2,1)} %bitcast.5, f32[1,512]{1,0:T(1,128)} %bitcast.6, ...), custom_call_target="tpu_custom_call" | custom-call | tf_op jit(solution)/shard_map/pallas_call | solution.py:395
  37.8 1.7 %copy.14 = bf16[2,128,512]{2,1,0:T(8,128)(2,1)} copy(bf16[2,128,512]{2,1,0:T(8,128)(2,1)} %shard_map.73) | data formatting | bytes 524288
Async XLA Ops:
  0.0 0.7 %copy-start = (f32[2,128,1]{1,2,0:T(1,128)S(1)}, f32[2,128,1]{1,2,0:T(1,128)}, u32[]{:S(2)}) copy-start(f32[2,128,1]{1,2,0:T(1,128)} %param.10) | copy-start | bytes 3076

commit v2 on v1

--- a/solution.py
+++ b/solution.py
@@ -195,7 +195,7 @@
     pl.semaphore_signal(barrier, inc=1, device_id=(me, opposite_head), device_id_type=MESH)
 
     tokens = key_ref.shape[1]
-    depth = weight_ref.shape[0]
+    parts, depth, _ = weight_ref.shape
     hd = key_ref.shape[2]
     size = kv_ref.shape[2]
 
@@ -203,9 +203,11 @@
         return pl.ds(pl.multiple_of(owner * count, count), count)
 
     own = rows(me, tokens)
-    w_buf[rows(me, depth)] = weight_ref[...]
+    for part in range(parts):
+        w_buf[rows(me, depth), part * hd : (part + 1) * hd] = weight_ref[part]
     k_buf[own] = key_ref[0]
-    s_buf[own] = (rate_ref[0] * value_ref[0].astype(jnp.float32)).astype(jnp.bfloat16)
+    rates = jnp.broadcast_to(rate_ref[0], (tokens, tokens)).T[:, :1]
+    s_buf[own] = (rates * value_ref[0].astype(jnp.float32)).astype(jnp.bfloat16)
     kv_buf[kind, :, own] = kv_ref[...]
 
     def part_of(item, owner):
@@ -275,19 +277,23 @@
         to_sibling(item, source)
 
     pl.semaphore_wait(barrier, 4)
-    for item in (0, 1, 2, 3):
+    for item in range(4):
         send(item, 0, near, 1)
+    for item in range(2):
         send(item, 0, far, 2)
+    for item in range(4):
         to_sibling(item, 0)
+    send_across(0)
+    for item in range(4):
+        pass_on(item, 1)
+        if item < 2:
+            send(item + 2, 0, far, 2)
         if item == 1:
-            send_across(0)
-
-    pass_on(0, 1)
+            send_across(1)
     pass_on(0, 2)
-    pass_on(1, 1)
-    send_across(1)
     pass_on(1, 2)
     send_across(2)
+    pass_on(2, 2)
     pass_on(0, 3)
     for slot in range(4, 8):
         arrived(0, slot)
@@ -322,10 +328,7 @@
     chip = me // 2
     arrived(2, 4)
     arrived(3, 4)
-    pass_on(2, 1)
-    pass_on(3, 1)
     terms(chip)
-    pass_on(2, 2)
     pass_on(3, 2)
     pass_on(1, 3)
     send_across(3)
@@ -389,7 +392,8 @@
     _, depth, parts, hd = fast_weights.shape
     _, tokens, size = key_value.shape
     length = members * tokens
-    weights = fast_weights[0].reshape(depth, parts * hd)
+    weights = jnp.swapaxes(fast_weights[0], 0, 1)
+    rates = jnp.swapaxes(fast_rate, 1, 2)
     sends = 4 * (members - 1) + members // 2
     bf16 = jnp.bfloat16
     return pl.pallas_call(
@@ -412,9 +416,9 @@
             pltpu.SemaphoreType.DMA((members // 2,)),
         ],
         compiler_params=pltpu.CompilerParams(
-            collective_id=0, has_side_effects=True, vmem_limit_bytes=56 * 1024 * 1024
+            collective_id=0, has_side_effects=True, vmem_limit_bytes=60 * 1024 * 1024
         ),
-    )(fast_query, fast_key, fast_value, fast_rate, weights, norm_gain[None], key_value)
+    )(fast_query, fast_key, fast_value, rates, weights, norm_gain[None], key_value)
 
 
 def solution(mesh):

time: 39.7 us -> 35.1 us (0.88)
  local copies, waits for them, and re-layouts: 4.97 us -> 1.67 us
  Pallas kernels: 34.5 us -> 33.2 us
    unnamed x6 -> x1, local copies, waits for them, and re-layouts: 4.97 us -> 1.67 us
    pallas_call x1, Pallas kernels: 34.5 us -> 33.2 us  [gathered_shards(): pl.pallas_call(whole_kernel, out_shape=jax.ShapeDtypeStruct(fast_query.sh...]
where the time goes in v2:
time: 35.1 us; the launch traced here: 34.9 us
  Pallas kernels  33.2 us (95%)
  local copies, waits for them, and re-layouts  1.67 us (5%)
    pallas_call x1, Pallas kernels, gathered_shards(): pl.pallas_call(whole_kernel, out_shape=jax.ShapeDtypeStruct(fast_query.sh...  33.2 us
    unnamed x1, local copies, waits for them, and re-layouts  1.67 us

profile of v2, /device:TPU:0, one launch (start us, length us, event | category | flops | bytes accessed | tf_op | source)
XLA Modules:
  0.0 34.9 jit_solution(9791687545503719893)
XLA Ops:
  0.0 33.2 %shard_map.73 = bf16[2,128,512]{2,1,0:T(8,128)(2,1)} custom-call(bf16[2,128,512]{2,1,0:T(8,128)(2,1)} %query_ref.1, bf16[2,128,512]{2,1,0:T(8,128)(2,1)} %key_ref.1, bf16[2,128,512]{2,1,0:T(8,128)(2,1)} %value_ref.1, f32[2,1,128]{2,1,0:T(1,128)} %bitcast.7, bf16[3,64,512]{2,1,0:T(8,128)(2,1)} %bitcast.5, f32[1,512]{1,0:T(1,128)} %bitcast.6, ...), custom_call_target="tpu_custom_call" | custom-call | tf_op jit(solution)/shard_map/pallas_call | solution.py:399
  33.2 1.7 %copy.9 = bf16[2,128,512]{2,1,0:T(8,128)(2,1)} copy(bf16[2,128,512]{2,1,0:T(8,128)(2,1)} %shard_map.73) | data formatting | bytes 524288

commit v3 on v2

--- a/solution.py
+++ b/solution.py
@@ -176,7 +176,7 @@
 
 def whole_kernel(
     query_ref, key_ref, value_ref, rate_ref, weight_ref, gain_ref, kv_ref, out_ref,
-    w_buf, k_buf, s_buf, kv_buf, hidden_buf, gates_buf, new_buf, merged,
+    w_buf, k_buf, s_buf, kv_buf, hidden_buf, gates_buf, new_buf, merged, grad_buf,
     send_sem, recv_sem, z_send, z_recv,
 ):
     me = lax.axis_index("tok")
@@ -325,11 +325,23 @@
         ).astype(jnp.bfloat16)
         gates_buf[span, hd:] = (backward * act).astype(jnp.bfloat16)
 
+    def gradient(chip):
+        span = rows(chip, 2 * tokens)
+        both = dot_along(k_buf[span], gates_buf[span], ALONG_ROWS)
+        down = dot_along(hidden_buf[span], s_buf[span], ALONG_ROWS)
+        return both, down
+
+    def accumulate(chip, first=False):
+        both, down = gradient(chip)
+        grad_buf[:, : 2 * hd] = both if first else grad_buf[:, : 2 * hd] + both
+        grad_buf[:, 2 * hd :] = down if first else grad_buf[:, 2 * hd :] + down
+
     chip = me // 2
     arrived(2, 4)
     arrived(3, 4)
     terms(chip)
     pass_on(3, 2)
+    accumulate(chip, first=True)
     pass_on(1, 3)
     send_across(3)
     for source in range(4):
@@ -339,7 +351,9 @@
         arrived(2, slot)
         arrived(3, slot)
     terms(chip ^ 1)
+    accumulate(chip ^ 1)
     terms(chip ^ 2)
+    accumulate(chip ^ 2)
     for slot in range(4, 8):
         arrived(1, slot)
         arrived(4, slot)
@@ -363,10 +377,10 @@
         factor = jnp.sqrt(jnp.mean(earlier * earlier, axis=-1, keepdims=True) + EPSILON) * rms(updated)
         new_buf[:, columns] = (updated * factor).astype(jnp.bfloat16)
 
-    both = dot_along(k_buf[...], gates_buf[...], ALONG_ROWS)
-    renewed(0, both[:, :hd])
-    renewed(1, both[:, hd:])
-    renewed(2, dot_along(hidden_buf[...], s_buf[...], ALONG_ROWS))
+    both, down = gradient(chip ^ 3)
+    renewed(0, grad_buf[:, :hd] + both[:, :hd])
+    renewed(1, grad_buf[:, hd : 2 * hd] + both[:, hd:])
+    renewed(2, grad_buf[:, 2 * hd :] + down)
 
     fast_second = applied(1, new_buf)
     for shard in range(length // tokens):
@@ -410,6 +424,7 @@
             pltpu.VMEM((length, 2 * hd), bf16),
             pltpu.VMEM((members * depth, parts * hd), bf16),
             pltpu.VMEM((2, length, size), bf16),
+            pltpu.VMEM((members * depth, parts * hd), jnp.float32),
             pltpu.SemaphoreType.DMA((sends,)),
             pltpu.SemaphoreType.DMA((5, members)),
             pltpu.SemaphoreType.DMA((members // 2,)),

time: 35.1 us -> 35.9 us (1.023)
  Pallas kernels: 33.2 us -> 34.1 us
    pallas_call x1, Pallas kernels: 33.2 us -> 34.1 us  [gathered_shards(): pl.pallas_call(whole_kernel, out_shape=jax.ShapeDtypeStruct(fast_query.sh...]
where the time goes in v3:
time: 35.9 us; the launch traced here: 35.8 us
  Pallas kernels  34.1 us (95%)
  local copies, waits for them, and re-layouts  1.67 us (5%)
    pallas_call x1, Pallas kernels, gathered_shards(): pl.pallas_call(whole_kernel, out_shape=jax.ShapeDtypeStruct(fast_query.sh...  34.1 us
    unnamed x1, local copies, waits for them, and re-layouts  1.67 us

profile of v3, /device:TPU:0, one launch (start us, length us, event | category | flops | bytes accessed | tf_op | source)
XLA Modules:
  0.0 35.8 jit_solution(11377326980032728504)
XLA Ops:
  0.0 34.1 %shard_map.73 = bf16[2,128,512]{2,1,0:T(8,128)(2,1)} custom-call(bf16[2,128,512]{2,1,0:T(8,128)(2,1)} %query_ref.1, bf16[2,128,512]{2,1,0:T(8,128)(2,1)} %key_ref.1, bf16[2,128,512]{2,1,0:T(8,128)(2,1)} %value_ref.1, f32[2,1,128]{2,1,0:T(1,128)} %bitcast.7, bf16[3,64,512]{2,1,0:T(8,128)(2,1)} %bitcast.5, f32[1,512]{1,0:T(1,128)} %bitcast.6, ...), custom_call_target="tpu_custom_call" | custom-call | tf_op jit(solution)/shard_map/pallas_call | solution.py:413
  34.1 1.7 %copy.9 = bf16[2,128,512]{2,1,0:T(8,128)(2,1)} copy(bf16[2,128,512]{2,1,0:T(8,128)(2,1)} %shard_map.73) | data formatting | bytes 524288
